TPU v7x, 32 devices: a whole 2x2x4 slice. The times are simulated.
32 devices in a mesh: row: 4 (over y, x), col: 8 (over z, core).
Axes of the slice: x: 2, y: 2, z: 4, core: 2. Of those that a mesh axis runs over, the one named last changes fastest.
Arguments:
- grad_out: bfloat16 [1536, 8192], P('row', 'col'), may hold values from -6 to 6
- gate_act: bfloat16 [1536, 28672], P('row', 'col'), may hold values from -6 to 6
- up_act: bfloat16 [1536, 28672], P('row', 'col'), may hold values from -6 to 6
- down_weight: bfloat16 [28672, 8192], P('col', 'row'), may hold values from -0.0625 to 0.0625
Outputs:
- grad_gate: bfloat16 [1536, 28672], P('row', 'col')
- grad_up: bfloat16 [1536, 28672], P('row', 'col')
- grad_weight: float32 [28672, 8192], P('col', 'row')
All inputs are finite; a program needn't handle non-finite values.
Results may differ from a plain program's by a relative error of at most 0.0028.
Values may be sent and summed in bfloat16 or wider, within the bound.
No kernel may reach another device: no remote copies, remote signals or barrier semaphores. Data moves between devices by JAX's collectives and lax.ppermute only.
A program may use at most 192 MiB of HBM per device.

v0:
```python
import jax
import jax.numpy as jnp
from jax import lax
from jax.sharding import PartitionSpec as P


def collect_features(grad_out):
    return lax.all_gather(grad_out, "col", axis=1, tiled=True)


def on_device(grad_out, gate_act, up_act, down_weight):
    token_major = lax.all_to_all(
        collect_features(grad_out), "row", split_axis=1, concat_axis=0, tiled=True
    )
    grad_rows = collect_features(grad_out)
    grad_hidden = lax.dot_general(
        grad_rows,
        lax.all_gather(down_weight, "row", axis=1, tiled=True),
        (((1,), (1,)), ((), ())),
        preferred_element_type=jnp.float32,
    )
    gate_value = gate_act.astype(jnp.float32)
    up_value = up_act.astype(jnp.float32)
    sigmoid_gate = jax.nn.sigmoid(gate_value)
    swish = gate_value * sigmoid_gate
    grad_gate = (
        grad_hidden * up_value * sigmoid_gate * (1.0 + gate_value * (1.0 - sigmoid_gate))
    ).astype(jnp.bfloat16)
    grad_up = (grad_hidden * swish).astype(jnp.bfloat16)
    hidden = (swish * up_value).astype(jnp.bfloat16)
    grad_weight = lax.dot_general(
        lax.all_gather(hidden, "row", axis=0, tiled=True),
        token_major,
        (((0,), (0,)), ((), ())),
        preferred_element_type=jnp.float32,
    )
    return (grad_gate, grad_up, grad_weight)


def solution(mesh):
    placed = (P("row", "col"), P("row", "col"), P("row", "col"), P("col", "row"))
    return jax.shard_map(
        on_device,
        mesh=mesh,
        in_specs=placed,
        out_specs=(P("row", "col"), P("row", "col"), P("col", "row")),
        check_vma=False,
    )
```

profile of v0, /device:TPU:0, one launch (start us, length us, event | category | flops | bytes accessed | tf_op | source)
XLA Modules:
  0.0 824.5 jit_solution(4998065232763771536)
XLA Ops:
  7.2 0.0 all-gather.4.cloned.1.call-start
  7.2 2.3 copy.7
  9.5 0.0 all-gather.4.cloned.1.call-update
  9.5 0.0 copy-start
  9.5 0.0 all-gather.6.cloned.1.call-start
  9.6 0.7 all-gather.6.cloned.1.call-update
  10.3 0.0 all-gather.8.cloned.1.call-start
  10.3 67.4 %all-gather.4.cloned.1.call-done = bf16[384,8192]{0,1:T(8,128)(2,1)} async-done(((bf16[384,1024]{0,1:T(8,128)(2,1)}), bf16[384,8192]{0,1:T(8,128)(2,1)}) %all-gather.4.cloned.1.call-update) | async-done | bytes 6291472 | tf_op jit(solution)/shard_map/all_gather | solution.py:8
  77.7 507.8 %all-gather.6.cloned.1.call-done = bf16[3584,8192]{1,0:T(8,128)(2,1)} async-done(((bf16[3584,2048]{1,0:T(8,128)(2,1)}), bf16[3584,8192]{1,0:T(8,128)(2,1)}) %all-gather.6.cloned.1.call-update) | async-done | bytes 58720272 | tf_op jit(solution)/shard_map/all_gather | solution.py:18
  585.5 0.0 copy-done
  585.5 32.8 %multiply_convert_fusion = (bf16[384,3584]{1,0:T(8,128)(2,1)}, bf16[384,3584]{1,0:T(8,128)(2,1)}, bf16[384,3584]{1,0:T(8,128)(2,1)}) fusion(bf16[384,3584]{1,0:T(8,128)(2,1)S(1)} %copy-done, bf16[384,3584]{1,0:T(8,128)(2,1)} %param.6, bf16[384,8192]{0,1:T(8,128)(2,1)} %all-gather.4.cloned.1.call-done, bf16[3584,8192]{1,0:T(8,128)(2,1)} %all-gather.6.cloned.1.call-done), kind=kOutput, calls=%fused_computation.13 | convolution fusion | flops 22571974656 | bytes 78774272 | tf_op jit(solution)/shard_map/dot_general | solution.py:16
  618.3 0.0 all-gather.8.cloned.1.call-update
  618.4 106.8 %all_to_all.19 = bf16[384,4,2048]{0,2,1:T(8,128)(2,1)} all-to-all(bf16[384,4,2048]{0,2,1:T(8,128)(2,1)} %bitcast.8), channel_id=1, replica_groups=mesh['row'=4,'col'=8] {'row'}, dimensions={1} | all-to-all | bytes 12582912 | tf_op jit(solution)/shard_map/all_to_all | solution.py:12
  725.2 8.6 %copy.8 = bf16[4,384,2048]{2,1,0:T(8,128)(2,1)} copy(bf16[4,384,2048]{1,2,0:T(8,128)(2,1)} %bitcast.7) | data formatting | bytes 12582912 | tf_op jit(solution)/shard_map/all_to_all | solution.py:12
  733.8 53.7 %all-gather.8.cloned.1.call-done = bf16[1536,3584]{1,0:T(8,128)(2,1)} async-done(((bf16[384,3584]{1,0:T(8,128)(2,1)}), bf16[1536,3584]{1,0:T(8,128)(2,1)}) %all-gather.8.cloned.1.call-update) | async-done | bytes 11010064 | tf_op jit(solution)/shard_map/all_gather | solution.py:32
  787.5 30.4 %fusion.8 = f32[3584,2048]{1,0:T(8,128)} fusion(bf16[1536,3584]{1,0:T(8,128)(2,1)} %all-gather.8.cloned.1.call-done, bf16[1536,2048]{1,0:T(8,128)(2,1)} %bitcast.9), kind=kOutput, calls=%fused_computation.14 | convolution fusion | flops 22548578304 | bytes 46661632 | tf_op jit(solution)/shard_map/dot_general | solution.py:31
Async XLA Ops:
  7.2 70.5 %all-gather.4.cloned.1.call-start = ((), (), s32[]{:S(2)}) async-start(), calls=%async_computation.1 | async-start | bytes 7077888 | tf_op jit(solution)/shard_map/all_gather | solution.py:8
  9.5 576.0 %copy-start = (bf16[384,3584]{1,0:T(8,128)(2,1)S(1)}, bf16[384,3584]{1,0:T(8,128)(2,1)}, u32[]{:S(2)}) copy-start(bf16[384,3584]{1,0:T(8,128)(2,1)} %param.5) | copy-start | bytes 8257540
  9.5 576.0 %all-gather.6.cloned.1.call-start = ((), (), s32[]{:S(2)}) async-start(), calls=%async_computation.2 | async-start | bytes 73400320 | tf_op jit(solution)/shard_map/all_gather | solution.py:18
  10.3 777.2 %all-gather.8.cloned.1.call-start = ((), (), s32[]{:S(2)}) async-start(), calls=%async_computation.3 | async-start | bytes 13762560 | tf_op jit(solution)/shard_map/all_gather | solution.py:32
Sparse Core Ops, SparseCore 0:
  10.2 67.4 all-gather.3
  79.6 505.9 all-gather.5
  618.5 168.9 all-gather.7
where the time goes:
time: 825 us; the launch traced here: 824 us
  waiting for transfers between devices  630 us (76%)
  blocking collectives  107 us (13%)
  matrix products  63.2 us (8%)
  between operations  13.8 us (2%)
  local copies, waits for them, and re-layouts  10.9 us (1%)
    all_gather x1, waiting for transfers between devices, on_device(): lax.all_gather(down_weight, 'row', axis=1, tiled=True)  508 us
    all_to_all x1, blocking collectives, on_device(): lax.all_to_all(collect_features(grad_out), 'row', split_axis=1, concat_ax...  107 us
    all_gather x1, waiting for transfers between devices, collect_features(): return lax.all_gather(grad_out, 'col', axis=1, tiled=True)  67.4 us
    all_gather x1, waiting for transfers between devices, on_device(): lax.all_gather(hidden, 'row', axis=0, tiled=True)  53.7 us
    dot_general x1, matrix products, on_device(): lax.dot_general(grad_rows, lax.all_gather(down_weight, 'row', axis=1, til...  32.8 us
    dot_general x1, matrix products, on_device(): lax.dot_general(lax.all_gather(hidden, 'row', axis=0, tiled=True), token_...  30.4 us
  transfers between devices with their start and end apart: 3, of which 3 were waited for; matrix products, arithmetic and copies ran while one was open for 1% of the time, Pallas kernels for 0%

commit v1 on v0

v1 whole, which is shorter than its diff:
```python
import jax
import jax.numpy as jnp
from jax import lax
from jax.sharding import PartitionSpec as P

CHUNKS = 4
BOTH = ("row", "col")


def exchange_pairs(rows, cols, step):
    bits = rows.bit_length() - 1
    return [
        (r * cols + c, (r ^ (1 << ((step + c) % bits))) * cols + c)
        for r in range(rows)
        for c in range(cols)
    ]


def token_order(rows, col_at):
    bits = rows.bit_length() - 1
    offsets = []
    for place in range(rows):
        offset = 0
        for step in range(bits):
            if place >> step & 1:
                offset = offset + (1 << ((step + col_at) % bits))
        offsets.append(offset)
    return offsets


def collect_tokens(grad_out, rows, cols):
    share = cols // rows
    part = grad_out.shape[0] // share
    lane = lax.axis_index("col") % share
    arrived = []
    for shift in range(share):
        piece = lax.dynamic_slice_in_dim(grad_out, (lane + shift) % share * part, part, 0)
        pairs = [
            (
                r * cols + to * share + k,
                to * cols + (r ^ to) * share + (k + shift) % share,
            )
            for r in range(rows)
            for to in range(rows)
            for k in range(share)
        ]
        arrived.append(lax.ppermute(piece, BOTH, pairs))
    arrived = jnp.stack(arrived)
    mine = jnp.concatenate(
        [
            lax.dynamic_index_in_dim(arrived, (lane - k) % share, 0, keepdims=False)
            for k in range(share)
        ],
        axis=1,
    )
    return lax.all_gather(mine, "col", axis=0, tiled=True)


def on_device(grad_out, gate_act, up_act, down_weight):
    rows, cols = lax.axis_size("row"), lax.axis_size("col")
    steps = rows.bit_length() - 1
    tokens = grad_out.shape[0]
    pairs = [exchange_pairs(rows, cols, step) for step in range(steps)]

    gate_value = gate_act.astype(jnp.float32)
    up_value = up_act.astype(jnp.float32)
    sigmoid_gate = jax.nn.sigmoid(gate_value)
    hidden = (gate_value * sigmoid_gate * up_value).astype(jnp.bfloat16)

    grads = collect_tokens(grad_out, rows, cols)
    offsets = token_order(rows, lax.axis_index("col"))
    places = sorted(
        range(rows), key=lambda place: [1 - (place >> step & 1) for step in range(steps)]
    )
    grads = jnp.concatenate(
        [
            lax.dynamic_slice_in_dim(grads, offsets[place] * tokens, tokens, 0)
            for place in places
        ],
        axis=0,
    )

    gathered = [hidden]
    for step in range(steps):
        gathered = gathered + [lax.ppermute(block, BOTH, pairs[step]) for block in gathered]
    hidden_all = jnp.concatenate([gathered[place] for place in places], axis=0)

    grads, gate_act, up_act, *_ = lax.optimization_barrier(
        (grads, gate_act, up_act, *gathered[1 : rows // 2 + 1])
    )
    grad_weight = lax.dot_general(
        hidden_all, grads, (((0,), (0,)), ((), ())), preferred_element_type=jnp.float32
    )

    width = down_weight.shape[0] // CHUNKS
    half = rows // 2 * tokens
    sums = []
    for chunk in range(CHUNKS):
        weight = lax.slice_in_dim(down_weight, chunk * width, (chunk + 1) * width, axis=0)

        def partial(start, stop):
            return lax.dot_general(
                grads[start:stop],
                weight,
                (((1,), (1,)), ((), ())),
                preferred_element_type=jnp.float32,
            )

        came = lax.ppermute(partial(0, half).astype(jnp.bfloat16), BOTH, pairs[0])
        if chunk == CHUNKS - 1:
            came, grad_weight = lax.optimization_barrier((came, grad_weight))
        if chunk == 0:
            grads, *_ = lax.optimization_barrier((grads, *gathered))
        start, arrived = half, [came]
        for step in range(1, steps):
            size = (rows * tokens - start) // 2
            total = partial(start, start + size)
            for block in arrived:
                total = total + block[:size].astype(jnp.float32)
            arrived = [block[size:] for block in arrived]
            arrived.append(lax.ppermute(total.astype(jnp.bfloat16), BOTH, pairs[step]))
            start += size
        total = partial(start, start + tokens)
        for block in arrived[:-1]:
            total = total + block.astype(jnp.float32)
        total, last = lax.optimization_barrier((total, arrived[-1]))
        sums.append(total + last.astype(jnp.float32))
    grad_hidden = jnp.concatenate(sums, axis=1)

    gate_value = gate_act.astype(jnp.float32)
    up_value = up_act.astype(jnp.float32)
    sigmoid_gate = jax.nn.sigmoid(gate_value)
    grad_gate = (
        grad_hidden * up_value * sigmoid_gate * (1.0 + gate_value * (1.0 - sigmoid_gate))
    ).astype(jnp.bfloat16)
    grad_up = (grad_hidden * (gate_value * sigmoid_gate)).astype(jnp.bfloat16)
    return (grad_gate, grad_up, grad_weight)


def solution(mesh):
    placed = (P("row", "col"), P("row", "col"), P("row", "col"), P("col", "row"))
    return jax.shard_map(
        on_device,
        mesh=mesh,
        in_specs=placed,
        out_specs=(P("row", "col"), P("row", "col"), P("col", "row")),
        check_vma=False,
    )
```

time: 825 us -> 286 us (0.35)
  waiting for transfers between devices: 630 us -> 84.9 us
  blocking collectives: 107 us -> 0 us
  starting transfers between devices: 0.12 us -> 88.4 us
  other arithmetic: 0 us -> 13.5 us
  matrix products: 63.2 us -> 75.5 us
    all_gather x3 -> x1, waiting for transfers between devices: 629 us -> 0.01 us  [collect_tokens(): return lax.all_gather(mine, 'col', axis=0, tiled=True)]
    all_to_all x1 -> x0, blocking collectives: 107 us -> none  [on_device(): lax.all_to_all(collect_features(grad_out), 'row', split_axis=1, concat_ax...]
    ppermute x0 -> x13, starting transfers between devices: none -> 88.4 us  [the longest x3 75.4 us: on_device(): lax.ppermute(block, BOTH, pairs[step])]
    ppermute x0 -> x13, waiting for transfers between devices: none -> 84.9 us  [the longest x3 51.3 us: on_device(): lax.ppermute(block, BOTH, pairs[step])]
    dot_general x2 -> x13, matrix products: 63.2 us -> 75.5 us  [the longest x12 46.5 us: partial(): lax.dot_general(grads[start:stop], weight, (((1,), (1,)), ((), ())), pref...]
    convert_element_type x0 -> x2, other arithmetic: none -> 9.28 us  [the longest x1 4.97 us: on_device(): hidden = (gate_value * sigmoid_gate * up_value).astype(jnp.bfloat16)]
    all_to_all x1 -> x0, local copies, waits for them, and re-layouts: 8.62 us -> none  [on_device(): lax.all_to_all(collect_features(grad_out), 'row', split_axis=1, concat_ax...]
  transfers between devices with their start and end apart: 3 -> 14, of which waited for: 3 -> 6; matrix products, arithmetic and copies ran while one was open for 1% -> 23% of each run, Pallas kernels for 0% -> 0%
where the time goes in v1:
time: 286 us; the launch traced here: 284 us
  starting transfers between devices  88.4 us (31%)
  waiting for transfers between devices  84.9 us (30%)
  matrix products  75.5 us (26%)
  between operations  14.3 us (5%)
  other arithmetic  13.5 us (5%)
  local copies, waits for them, and re-layouts  7.05 us (2%)
    ppermute x3, starting transfers between devices, on_device(): lax.ppermute(block, BOTH, pairs[step])  75.4 us
    ppermute x3, waiting for transfers between devices, on_device(): lax.ppermute(block, BOTH, pairs[step])  51.3 us
    dot_general x12, matrix products, partial(): lax.dot_general(grads[start:stop], weight, (((1,), (1,)), ((), ())), pref...  46.5 us
    ppermute x4, waiting for transfers between devices, on_device(): came = lax.ppermute(partial(0, half).astype(jnp.bfloat16), BOTH, pairs[0])  31.3 us
    dot_general x1, matrix products, on_device(): lax.dot_general(hidden_all, grads, (((0,), (0,)), ((), ())), preferred_el...  29.1 us
    ppermute x4, starting transfers between devices, on_device(): arrived.append(lax.ppermute(total.astype(jnp.bfloat16), BOTH, pairs[step]))  6.77 us
  transfers between devices with their start and end apart: 14, of which 6 were waited for; matrix products, arithmetic and copies ran while one was open for 23% of the time, Pallas kernels for 0%

profile of v1, /device:TPU:0, one launch (start us, length us, event | category | flops | bytes accessed | tf_op | source)
XLA Modules:
  0.0 283.7 jit_solution(5945502851630634559)
XLA Ops:
  7.2 0.0 all-gather.2.cloned.1.call-start
  7.3 2.1 constant_dynamic-slice_fusion.3
  9.3 1.6 collective-permute-start
  11.0 0.5 collective-permute-start.1
  11.4 1.5 collective-permute-done.1
  12.9 1.3 fusion.96
  14.2 0.9 pad_maximum_fusion.2
  15.1 0.0 all-gather.2.cloned.1.call-update
  15.2 5.0 %fusion.20 = bf16[384,3584]{1,0:T(8,128)(2,1)} fusion(bf16[384,3584]{1,0:T(8,128)(2,1)} %param.6, bf16[384,3584]{1,0:T(8,128)(2,1)S(1)} %copy-done), kind=kLoop, calls=%fused_computation.27 | loop fusion | flops 11010048 | bytes 8257536 | tf_op jit(solution)/shard_map/convert_element_type | solution.py:68
  20.1 19.8 %collective-permute-start.2 = (bf16[384,3584]{1,0:T(8,128)(2,1)}, bf16[384,3584]{1,0:T(8,128)(2,1)}, u32[]{:S(2)}, u32[]{:S(2)}) collective-permute-start(bf16[384,3584]{1,0:T(8,128)(2,1)} %fusion.20), channel_id=1, source_target_pairs={{0,8},{1,17},{2,10},{3,19},{4,12},{5,21},{6,14},{7,23},{8,0},{9,25... | collective-permute-start | bytes 8257544 | tf_op jit(solution)/shard_map/ppermute | solution.py:85
  39.9 17.7 %collective-permute-start.3 = (bf16[384,3584]{1,0:T(8,128)(2,1)}, bf16[384,3584]{1,0:T(8,128)(2,1)}, u32[]{:S(2)}, u32[]{:S(2)}) collective-permute-start(bf16[384,3584]{1,0:T(8,128)(2,1)} %fusion.20), channel_id=1, source_target_pairs={{0,16},{1,9},{2,18},{3,11},{4,20},{5,13},{6,22},{7,15},{8,24},{9,1... | collective-permute-start | bytes 8257544 | tf_op jit(solution)/shard_map/ppermute | solution.py:85
  57.6 24.9 %collective-permute-done.2 = bf16[384,3584]{1,0:T(8,128)(2,1)} collective-permute-done((bf16[384,3584]{1,0:T(8,128)(2,1)}, bf16[384,3584]{1,0:T(8,128)(2,1)}, u32[]{:S(2)}, u32[]{:S(2)}) %collective-permute-start.2) | collective-permute-done | bytes 2752544 | tf_op jit(solution)/shard_map/ppermute | solution.py:85
  82.6 37.9 %collective-permute-start.4 = (bf16[384,3584]{1,0:T(8,128)(2,1)}, bf16[384,3584]{1,0:T(8,128)(2,1)}, u32[]{:S(2)}, u32[]{:S(2)}) collective-permute-start(bf16[384,3584]{1,0:T(8,128)(2,1)} %collective-permute-done.2), channel_id=1, source_target_pairs={{0,16},{1,9},{2,18},{3,11},{4,20},{5,13},{6,22},{7,15},{8,24},{9,1... | collective-permute-start | bytes 8257544 | tf_op jit(solution)/shard_map/ppermute | solution.py:85
  120.5 3.4 %constant_dynamic-slice_fusion.2 = (bf16[384,2048]{1,0:T(8,128)(2,1)S(1)}, bf16[384,2048]{1,0:T(8,128)(2,1)S(1)}, bf16[384,2048]{1,0:T(8,128)(2,1)S(1)}, bf16[384,2048]{1,0:T(8,128)(2,1)S(1)}) fusion(bf16[1536,2048]{1,0:T(8,128)(2,1)} %all-gather.2.cloned.1.call-done, s32[]{:T(128)S(6)} %select_n.62, s32[]{:T(128)S(6)} %select_n.64, s32[]{:T(128)S(6)} %select_n.63), kind=kLoop, calls=%fused_computation.91 | loop fusion | bytes 12582924 | tf_op jit(solution)/shard_map/dynamic_slice | solution.py:77
  123.9 1.5 pad_maximum_fusion
  125.4 0.0 collective-permute-done.3
  125.4 26.4 %collective-permute-done.4 = bf16[384,3584]{1,0:T(8,128)(2,1)} collective-permute-done((bf16[384,3584]{1,0:T(8,128)(2,1)}, bf16[384,3584]{1,0:T(8,128)(2,1)}, u32[]{:S(2)}, u32[]{:S(2)}) %collective-permute-start.4) | collective-permute-done | bytes 2752544 | tf_op jit(solution)/shard_map/ppermute | solution.py:85
  151.8 6.9 %fusion.59 = bf16[768,896]{1,0:T(8,128)(2,1)} fusion(bf16[3584,2048]{1,0:T(8,128)(2,1)} %param.7, bf16[1536,2048]{1,0:T(8,128)(2,1)S(1)} %pad_maximum_fusion), kind=kOutput, calls=%fused_computation.58 | convolution fusion | flops 2819260416 | bytes 8192000 | tf_op jit(solution)/shard_map/dot_general | solution.py:102
  158.7 6.9 %fusion.54 = bf16[768,896]{1,0:T(8,128)(2,1)} fusion(bf16[3584,2048]{1,0:T(8,128)(2,1)} %param.7, bf16[1536,2048]{1,0:T(8,128)(2,1)S(1)} %pad_maximum_fusion), kind=kOutput, calls=%fused_computation.57 | convolution fusion | flops 2819260416 | bytes 8192000 | tf_op jit(solution)/shard_map/dot_general | solution.py:102
  165.7 3.5 %fusion.49 = bf16[768,896]{1,0:T(8,128)(2,1)S(1)} fusion(bf16[3584,2048]{1,0:T(8,128)(2,1)S(1)} %bitcast.9, bf16[1536,2048]{1,0:T(8,128)(2,1)S(1)} %pad_maximum_fusion), kind=kOutput, calls=%fused_computation.56 | convolution fusion | flops 2819260416 | bytes 8192000 | tf_op jit(solution)/shard_map/dot_general | solution.py:102
  169.1 3.5 %fusion.64 = bf16[768,896]{1,0:T(8,128)(2,1)S(1)} fusion(bf16[3584,2048]{1,0:T(8,128)(2,1)S(1)} %bitcast.9, bf16[1536,2048]{1,0:T(8,128)(2,1)S(1)} %pad_maximum_fusion), kind=kOutput, calls=%fused_computation.59 | convolution fusion | flops 2819260416 | bytes 8192000 | tf_op jit(solution)/shard_map/dot_general | solution.py:102
  172.6 0.1 collective-permute-start.11
  172.7 2.0 collective-permute-start.9
  174.7 0.1 collective-permute-start.7
  174.8 1.9 collective-permute-start.5
  176.7 29.1 %fusion = f32[3584,2048]{1,0:T(8,128)} fusion(bf16[1536,2048]{1,0:T(8,128)(2,1)S(1)} %pad_maximum_fusion, bf16[384,3584]{1,0:T(8,128)(2,1)} %fusion.20, bf16[384,3584]{1,0:T(8,128)(2,1)} %collective-permute-done.3, bf16[384,3584]{1,0:T(8,128)(2,1)} %collective-permute-done.2, bf16[384,3584]{1,0:T(8,128)(2,1)} %collective-permute-done.4), kind=kOutput, calls=%fused_computation | convolution fusion | flops 22592618496 | bytes 46661632 | tf_op jit(solution)/shard_map/dot_general | solution.py:91
  205.8 0.0 slice-start.5
  205.8 5.0 %add_convert_fusion = bf16[384,896]{1,0:T(8,128)(2,1)} fusion(bf16[3584,2048]{1,0:T(8,128)(2,1)} %param.7, bf16[1536,2048]{1,0:T(8,128)(2,1)S(1)} %pad_maximum_fusion, bf16[768,896]{1,0:T(8,128)(2,1)S(1)} %collective-permute-done.11), kind=kOutput, calls=%fused_computation.61 | convolution fusion | flops 1410318336 | bytes 6619136 | tf_op jit(solution)/shard_map/dot_general | solution.py:102
  210.8 2.0 collective-permute-start.12
  212.9 4.9 %add_convert_fusion.1 = bf16[384,896]{1,0:T(8,128)(2,1)} fusion(bf16[3584,2048]{1,0:T(8,128)(2,1)} %param.7, bf16[1536,2048]{1,0:T(8,128)(2,1)S(1)} %pad_maximum_fusion, bf16[768,896]{1,0:T(8,128)(2,1)S(1)} %collective-permute-done.9), kind=kOutput, calls=%fused_computation.64 | convolution fusion | flops 1410318336 | bytes 6619136 | tf_op jit(solution)/shard_map/dot_general | solution.py:102
  217.7 0.2 collective-permute-start.10
  217.9 11.3 %collective-permute-done.7 = bf16[768,896]{1,0:T(8,128)(2,1)S(1)} collective-permute-done((bf16[768,896]{1,0:T(8,128)(2,1)S(1)}, bf16[768,896]{1,0:T(8,128)(2,1)S(1)}, u32[]{:S(2)}, u32[]{:S(2)}) %collective-permute-start.7) | collective-permute-done | bytes 1376288 | tf_op jit(solution)/shard_map/ppermute | solution.py:109
  229.2 4.0 %add_convert_fusion.2 = bf16[384,896]{1,0:T(8,128)(2,1)S(1)} fusion(bf16[3584,2048]{1,0:T(8,128)(2,1)} %param.7, bf16[1536,2048]{1,0:T(8,128)(2,1)S(1)} %pad_maximum_fusion, bf16[768,896]{1,0:T(8,128)(2,1)S(1)} %collective-permute-done.7), kind=kOutput, calls=%fused_computation.67 | convolution fusion | flops 1410318336 | bytes 6619136 | tf_op jit(solution)/shard_map/dot_general | solution.py:102
  233.2 2.5 collective-permute-start.8
  235.6 1.9 convert_add_fusion.1
  237.5 20.0 %collective-permute-done.5 = bf16[768,896]{1,0:T(8,128)(2,1)S(1)} collective-permute-done((bf16[768,896]{1,0:T(8,128)(2,1)S(1)}, bf16[768,896]{1,0:T(8,128)(2,1)S(1)}, u32[]{:S(2)}, u32[]{:S(2)}) %collective-permute-start.5) | collective-permute-done | bytes 1376288 | tf_op jit(solution)/shard_map/ppermute | solution.py:109
  257.5 1.9 add_convert_fusion.3
  259.4 2.1 collective-permute-start.6
  261.6 1.9 convert_add_fusion.3
  263.5 2.2 convert_add_fusion.5
  265.7 4.0 %convert_add_fusion.7 = f32[384,896]{1,0:T(8,128)S(1)} fusion(bf16[3584,2048]{1,0:T(8,128)(2,1)} %param.7, bf16[1536,2048]{1,0:T(8,128)(2,1)S(1)} %pad_maximum_fusion, bf16[768,896]{1,0:T(8,128)(2,1)S(1)} %collective-permute-done.5), kind=kOutput, calls=%fused_computation.71 | convolution fusion | flops 1409974272 | bytes 7307264 | tf_op jit(solution)/shard_map/dot_general | solution.py:102
  269.7 0.0 collective-permute-done.12
  269.7 0.8 collective-permute-done.6
  270.5 0.2 convert_add_fusion
  270.7 0.0 copy-start.1
  270.7 0.2 convert_add_fusion.4
  271.0 1.5 copy-done.1
  272.5 4.3 %fusion.19 = (bf16[384,3584]{1,0:T(8,128)(2,1)}, bf16[384,3584]{1,0:T(8,128)(2,1)}) fusion(bf16[384,3584]{1,0:T(8,128)(2,1)S(1)} %copy-done, f32[384,896]{1,0:T(8,128)S(1)} %get-tuple-element.41, f32[384,896]{1,0:T(8,128)S(1)} %get-tuple-element.42, f32[384,896]{1,0:T(8,128)S(1)} %get-tuple-element.43, f32[384,896]{1,0:T(8,128)S(1)} %get-tuple-element.44, ...), kind=kLoop, calls=%fused_computation.25 | loop fusion | flops 24772608 | bytes 16515072 | tf_op jit(solution)/shard_map/convert_element_type | solution.py:136
  (25 shorter events, 0.0 us)
Async XLA Ops:
  7.2 8.0 %copy-start = (bf16[384,3584]{1,0:T(8,128)(2,1)S(1)}, bf16[384,3584]{1,0:T(8,128)(2,1)}, u32[]{:S(2)}) copy-start(bf16[384,3584]{1,0:T(8,128)(2,1)} %param.5) | copy-start | bytes 8257540
  7.2 113.3 %all-gather.2.cloned.1.call-start = ((), (), s32[]{:S(2)}) async-start(), calls=%async_computation | async-start | bytes 7077888 | tf_op jit(solution)/shard_map/all_gather | solution.py:56
  9.3 2.1 collective-permute-start
  11.0 1.9 collective-permute-start.1
  20.1 62.4 %collective-permute-start.2 = (bf16[384,3584]{1,0:T(8,128)(2,1)}, bf16[384,3584]{1,0:T(8,128)(2,1)}, u32[]{:S(2)}, u32[]{:S(2)}) collective-permute-start(bf16[384,3584]{1,0:T(8,128)(2,1)} %fusion.20), channel_id=1, source_target_pairs={{0,8},{1,17},{2,10},{3,19},{4,12},{5,21},{6,14},{7,23},{8,0},{9,25... | collective-permute-start | bytes 8257544 | tf_op jit(solution)/shard_map/ppermute | solution.py:85
  39.9 85.5 %collective-permute-start.3 = (bf16[384,3584]{1,0:T(8,128)(2,1)}, bf16[384,3584]{1,0:T(8,128)(2,1)}, u32[]{:S(2)}, u32[]{:S(2)}) collective-permute-start(bf16[384,3584]{1,0:T(8,128)(2,1)} %fusion.20), channel_id=1, source_target_pairs={{0,16},{1,9},{2,18},{3,11},{4,20},{5,13},{6,22},{7,15},{8,24},{9,1... | collective-permute-start | bytes 8257544 | tf_op jit(solution)/shard_map/ppermute | solution.py:85
  82.6 69.3 %collective-permute-start.4 = (bf16[384,3584]{1,0:T(8,128)(2,1)}, bf16[384,3584]{1,0:T(8,128)(2,1)}, u32[]{:S(2)}, u32[]{:S(2)}) collective-permute-start(bf16[384,3584]{1,0:T(8,128)(2,1)} %collective-permute-done.2), channel_id=1, source_target_pairs={{0,16},{1,9},{2,18},{3,11},{4,20},{5,13},{6,22},{7,15},{8,24},{9,1... | collective-permute-start | bytes 8257544 | tf_op jit(solution)/shard_map/ppermute | solution.py:85
  151.8 13.8 %slice-start = ((s8[14680064]{0:T(1024)(128)(4,1)}), s8[4194304]{0:T(1024)(128)(4,1)S(1)}, s32[]{:S(2)}) async-start(s8[14680064]{0:T(1024)(128)(4,1)} %bitcast.8), calls=%async_computation.1 | async-start | bytes 8388608
  151.8 13.8 %slice-start.1 = ((s8[14680064]{0:T(1024)(128)(4,1)}), s8[4194304]{0:T(1024)(128)(4,1)S(1)}, s32[]{:S(2)}) async-start(s8[14680064]{0:T(1024)(128)(4,1)} %bitcast.8), calls=%async_computation.2 | async-start | bytes 8388608
  158.7 6.9 %slice-start.2 = ((s8[14680064]{0:T(1024)(128)(4,1)}), s8[4194304]{0:T(1024)(128)(4,1)S(1)}, s32[]{:S(2)}) async-start(s8[14680064]{0:T(1024)(128)(4,1)} %bitcast.8), calls=%async_computation.3 | async-start | bytes 8388608
  158.7 6.9 %slice-start.3 = ((s8[14680064]{0:T(1024)(128)(4,1)}), s8[2097152]{0:T(1024)(128)(4,1)S(1)}, s32[]{:S(2)}) async-start(s8[14680064]{0:T(1024)(128)(4,1)} %bitcast.8), calls=%async_computation.4 | async-start | bytes 4194304
  172.6 33.2 %collective-permute-start.11 = (bf16[768,896]{1,0:T(8,128)(2,1)}, bf16[768,896]{1,0:T(8,128)(2,1)S(1)}, u32[]{:S(2)}, u32[]{:S(2)}) collective-permute-start(bf16[768,896]{1,0:T(8,128)(2,1)} %fusion.59), channel_id=1, source_target_pairs={{0,8},{1,17},{2,10},{3,19},{4,12},{5,21},{6,14},{7,23},{8,0},{9,25... | collective-permute-start | bytes 4128776 | tf_op jit(solution)/shard_map/ppermute | solution.py:109
  172.7 40.2 %collective-permute-start.9 = (bf16[768,896]{1,0:T(8,128)(2,1)}, bf16[768,896]{1,0:T(8,128)(2,1)S(1)}, u32[]{:S(2)}, u32[]{:S(2)}) collective-permute-start(bf16[768,896]{1,0:T(8,128)(2,1)} %fusion.54), channel_id=1, source_target_pairs={{0,8},{1,17},{2,10},{3,19},{4,12},{5,21},{6,14},{7,23},{8,0},{9,25... | collective-permute-start | bytes 4128776 | tf_op jit(solution)/shard_map/ppermute | solution.py:109
  174.7 54.5 %collective-permute-start.7 = (bf16[768,896]{1,0:T(8,128)(2,1)S(1)}, bf16[768,896]{1,0:T(8,128)(2,1)S(1)}, u32[]{:S(2)}, u32[]{:S(2)}) collective-permute-start(bf16[768,896]{1,0:T(8,128)(2,1)S(1)} %fusion.49), channel_id=1, source_target_pairs={{0,8},{1,17},{2,10},{3,19},{4,12},{5,21},{6,14},{7,23},{8,0},{9,25... | collective-permute-start | bytes 4128776 | tf_op jit(solution)/shard_map/ppermute | solution.py:109
  174.8 82.8 %collective-permute-start.5 = (bf16[768,896]{1,0:T(8,128)(2,1)S(1)}, bf16[768,896]{1,0:T(8,128)(2,1)S(1)}, u32[]{:S(2)}, u32[]{:S(2)}) collective-permute-start(bf16[768,896]{1,0:T(8,128)(2,1)S(1)} %fusion.64), channel_id=1, source_target_pairs={{0,8},{1,17},{2,10},{3,19},{4,12},{5,21},{6,14},{7,23},{8,0},{9,25... | collective-permute-start | bytes 4128776 | tf_op jit(solution)/shard_map/ppermute | solution.py:109
  205.8 29.8 %slice-start.4 = ((s8[14680064]{0:T(1024)(128)(4,1)}), s8[4194304]{0:T(1024)(128)(4,1)S(1)}, s32[]{:S(2)}) async-start(s8[14680064]{0:T(1024)(128)(4,1)} %bitcast.10), calls=%async_computation.5 | async-start | bytes 8388608
  205.8 29.8 %slice-start.5 = ((s8[14680064]{0:T(1024)(128)(4,1)}), s8[4194304]{0:T(1024)(128)(4,1)S(1)}, s32[]{:S(2)}) async-start(s8[14680064]{0:T(1024)(128)(4,1)} %bitcast.10), calls=%async_computation.6 | async-start | bytes 8388608
  210.8 24.8 %slice-start.6 = ((s8[14680064]{0:T(1024)(128)(4,1)}), s8[4194304]{0:T(1024)(128)(4,1)S(1)}, s32[]{:S(2)}) async-start(s8[14680064]{0:T(1024)(128)(4,1)} %bitcast.10), calls=%async_computation.7 | async-start | bytes 8388608
  210.8 58.8 %collective-permute-start.12 = (bf16[384,896]{1,0:T(8,128)(2,1)}, bf16[384,896]{1,0:T(8,128)(2,1)S(1)}, u32[]{:S(2)}, u32[]{:S(2)}) collective-permute-start(bf16[384,896]{1,0:T(8,128)(2,1)} %add_convert_fusion), channel_id=1, source_target_pairs={{0,16},{1,9},{2,18},{3,11},{4,20},{5,13},{6,22},{7,15},{8,24},{9,1... | collective-permute-start | bytes 2064392 | tf_op jit(solution)/shard_map/ppermute | solution.py:121
  217.7 17.9 %slice-start.7 = ((s8[14680064]{0:T(1024)(128)(4,1)}), s8[2097152]{0:T(1024)(128)(4,1)S(1)}, s32[]{:S(2)}) async-start(s8[14680064]{0:T(1024)(128)(4,1)} %bitcast.10), calls=%async_computation.8 | async-start | bytes 4194304
  217.7 52.0 %collective-permute-start.10 = (bf16[384,896]{1,0:T(8,128)(2,1)}, bf16[384,896]{1,0:T(8,128)(2,1)S(1)}, u32[]{:S(2)}, u32[]{:S(2)}) collective-permute-start(bf16[384,896]{1,0:T(8,128)(2,1)} %add_convert_fusion.1), channel_id=1, source_target_pairs={{0,16},{1,9},{2,18},{3,11},{4,20},{5,13},{6,22},{7,15},{8,24},{9,1... | collective-permute-start | bytes 2064392 | tf_op jit(solution)/shard_map/ppermute | solution.py:121
  233.2 36.5 %collective-permute-start.8 = (bf16[384,896]{1,0:T(8,128)(2,1)S(1)}, bf16[384,896]{1,0:T(8,128)(2,1)S(1)}, u32[]{:S(2)}, u32[]{:S(2)}) collective-permute-start(bf16[384,896]{1,0:T(8,128)(2,1)S(1)} %add_convert_fusion.2), channel_id=1, source_target_pairs={{0,16},{1,9},{2,18},{3,11},{4,20},{5,13},{6,22},{7,15},{8,24},{9,1... | collective-permute-start | bytes 2064392 | tf_op jit(solution)/shard_map/ppermute | solution.py:121
  259.4 11.0 %collective-permute-start.6 = (bf16[384,896]{1,0:T(8,128)(2,1)S(1)}, bf16[384,896]{1,0:T(8,128)(2,1)S(1)}, u32[]{:S(2)}, u32[]{:S(2)}) collective-permute-start(bf16[384,896]{1,0:T(8,128)(2,1)S(1)} %add_convert_fusion.3), channel_id=1, source_target_pairs={{0,16},{1,9},{2,18},{3,11},{4,20},{5,13},{6,22},{7,15},{8,24},{9,1... | collective-permute-start | bytes 2064392 | tf_op jit(solution)/shard_map/ppermute | solution.py:121
  270.7 1.8 copy-start.1
Sparse Core Ops, SparseCore 0:
  15.3 102.8 all-gather.1
